TPU v7x, 128 devices: a whole 4x4x4 slice. The times are simulated.
128 devices in a mesh: rep: 16 (over x, z), tp: 8 (over y, core).
Axes of the slice: x: 4, y: 4, z: 4, core: 2. Of those that a mesh axis runs over, the one named last changes fastest.
Arguments:
- hidden: bfloat16 [16384, 8192], P('rep', 'tp'), may hold values from -6 to 6
- w_query: bfloat16 [8192, 4096], P(None, 'tp'), may hold values from -1 to 1
- w_keyval: bfloat16 [8192, 2048], P(None, 'tp'), may hold values from -1 to 1
- kv_pool: bfloat16 [2048, 128, 2048], P('rep', None, 'tp'), may hold values from -240 to 240
- prefix_len: int32 [128], replicated, may hold values from 1 to 2048, 65536 in all
- owner: int32 [128], replicated, may hold values from 0 to 15, as said below
- block_table: int32 [128, 16], replicated, may hold values from 0 to 127, as said below
Outputs:
- attended: bfloat16 [16384, 4096], P('rep', 'tp')
- new_cache: bfloat16 [128, 128, 2048], P('rep', None, 'tp')
Inputs may be any that keep to these rules, and one draw needn't show every extreme that they name: `owner`: the 8 spans of one replica (entries r * 8 onward) have distinct owners, and every replica owns exactly one span c with c % 8 == k for each k. `block_table`: each row lists distinct pages of the owner's pool; the rows of the spans one replica owns use every page of its pool exactly once.
All inputs are finite; a program needn't handle non-finite values.
Results may differ from a plain program's by a relative error of at most 0.011.
Values may be sent and summed in bfloat16 or wider, within the bound.
A program may use at most 192 MiB of HBM per device.

v0:
```python
import math

import jax
import jax.numpy as jnp
from jax import lax
from jax.sharding import PartitionSpec as P

HEAD_DIM = 128
SPAN_LEN = 128


ROPE_BASE = 500000.0


def rotate(values, positions):
    half_dim = values.shape[-1] // 2
    frequency = ROPE_BASE ** (-jnp.arange(half_dim, dtype=jnp.float32) * 2.0 / values.shape[-1])
    angles = positions.astype(jnp.float32)[..., None] * frequency
    cosine = jnp.cos(angles)
    sine_part = jnp.sin(angles)
    front = values[..., :half_dim]
    back_half = values[..., half_dim:]
    return jnp.concatenate(
        [front * cosine - back_half * sine_part, back_half * cosine + front * sine_part], axis=-1
    )


def attend_one(queries, keys, values, visible):
    scale_factor = 1.0 / math.sqrt(queries.shape[-1])
    scores = (
        jnp.einsum("ckgd,skd->ckgs", queries, keys, preferred_element_type=jnp.float32)
        * scale_factor
    )
    scores = jnp.where(visible[:, None, None, :], scores, -jnp.inf)
    highest = jnp.max(scores, axis=-1)
    weights = jnp.exp(scores - highest[..., None])
    totals = jnp.sum(weights, axis=-1)
    summed = jnp.einsum(
        "ckgs,skd->ckgd", weights.astype(jnp.bfloat16), values, preferred_element_type=jnp.float32
    )
    return (summed, highest, totals)


def attend_part(queries, keys, values, visible):
    return lax.map(
        lambda items: attend_one(items[0], items[1], items[2], items[3]),
        (queries, keys, values, visible),
    )


def combine_parts(first, second):
    top_value = jnp.maximum(first[1], second[1])
    scale_one = jnp.exp(first[1] - top_value)
    scale_two = jnp.exp(second[1] - top_value)
    summed = first[0] * scale_one[..., None] + second[0] * scale_two[..., None]
    return summed / (first[2] * scale_one + second[2] * scale_two)[..., None]


def body(hidden, w_query, w_keyval, kv_pool, prefix_len, owner, block_table):
    replicas = lax.axis_size("rep")
    own_index = lax.axis_index("rep")
    tokens_dev = hidden.shape[0]
    per_device = tokens_dev // SPAN_LEN
    piece = lax.all_gather(hidden, "tp", axis=1, tiled=True)
    query = jnp.dot(piece, w_query, preferred_element_type=jnp.float32)
    keyval = jnp.dot(piece, w_keyval, preferred_element_type=jnp.float32)
    kv_local = w_keyval.shape[1] // (2 * HEAD_DIM)
    group = w_query.shape[1] // HEAD_DIM // kv_local
    width = 2 * HEAD_DIM * kv_local
    offsets = jnp.arange(SPAN_LEN, dtype=jnp.int32)
    lengths_mine = lax.dynamic_slice_in_dim(prefix_len, own_index * per_device, per_device, 0)
    targets = lax.dynamic_slice_in_dim(owner, own_index * per_device, per_device, 0)
    positions = lengths_mine[:, None] + offsets[None, :]
    query = query.reshape(per_device, SPAN_LEN, kv_local * group, HEAD_DIM)
    q_rot = rotate(query, positions[:, :, None]).astype(jnp.bfloat16)
    q_groups = q_rot.reshape(per_device, SPAN_LEN, kv_local, group, HEAD_DIM)
    keyval = keyval.reshape(per_device, SPAN_LEN, kv_local, 2 * HEAD_DIM)
    fresh = jnp.concatenate(
        [rotate(keyval[..., :HEAD_DIM], positions[:, :, None]), keyval[..., HEAD_DIM:]], axis=-1
    ).astype(jnp.bfloat16)
    causal = jnp.broadcast_to(
        offsets[:, None] >= offsets[None, :], (per_device, SPAN_LEN, SPAN_LEN)
    )
    local_part = attend_part(q_groups, fresh[..., :HEAD_DIM], fresh[..., HEAD_DIM:], causal)
    matches = (owner.reshape(replicas, per_device) == own_index).astype(jnp.int32)
    sources = jnp.sum(jnp.arange(replicas, dtype=jnp.int32)[:, None] * matches, axis=0)
    owned = sources * per_device + jnp.arange(per_device, dtype=jnp.int32)
    owned_prefix = kv_pool[block_table[owned]].reshape(per_device, -1, kv_local, 2 * HEAD_DIM)
    prefix_span = owned_prefix.shape[1]
    span_index = jnp.arange(prefix_span, dtype=jnp.int32)
    fresh_send = (
        jnp.zeros((replicas, SPAN_LEN, width), jnp.bfloat16)
        .at[targets]
        .set(fresh.reshape(per_device, SPAN_LEN, width))
    )
    prefix_send = (
        jnp.zeros((replicas, prefix_span, kv_local, 2 * HEAD_DIM), jnp.bfloat16)
        .at[sources]
        .set(owned_prefix)
    )
    prefix_recv = lax.all_to_all(prefix_send, "rep", split_axis=0, concat_axis=0, tiled=True)
    fresh_recv = lax.all_to_all(fresh_send, "rep", split_axis=0, concat_axis=0, tiled=True)
    prefix_mine = prefix_recv[targets]
    visible = jnp.broadcast_to(
        (span_index[None, :] < lengths_mine[:, None])[:, None, :],
        (per_device, SPAN_LEN, prefix_span),
    )
    remote_part = attend_part(
        q_groups, prefix_mine[..., :HEAD_DIM], prefix_mine[..., HEAD_DIM:], visible
    )
    attended = combine_parts(local_part, remote_part).reshape(tokens_dev, -1).astype(jnp.bfloat16)
    new_cache = fresh_recv[sources]
    return (attended, new_cache)


def solution(mesh):
    placed = (P("rep", "tp"), P(None, "tp"), P(None, "tp"), P("rep", None, "tp"), P(), P(), P())
    return jax.shard_map(
        body,
        mesh=mesh,
        in_specs=placed,
        out_specs=(P("rep", "tp"), P("rep", None, "tp")),
        check_vma=False,
    )
```

profile of v0, /device:TPU:0, one launch (start us, length us, event | category | flops | bytes accessed | tf_op | source)
XLA Modules:
  0.0 494.6 jit_solution(6271560495224052881)
XLA Ops:
  7.2 0.7 all-gather.2.cloned.1.call-update
  7.9 0.7 broadcast_compare_fusion
  8.7 0.8 copy.44
  10.2 10.0 %gather_fusion.1 = bf16[128,128,256]{2,1,0:T(8,128)(2,1)} fusion(bf16[128,128,256]{2,1,0:T(8,128)(2,1)} %param.14, s32[1024]{0:T(1024)S(1)} %pad_clamp_fusion.2), kind=kCustom, calls=%fused_computation.1 | custom fusion | bytes 16777728 | tf_op jit(solution)/shard_map/gather | solution.py:88
  20.1 8.0 %broadcast.181 = bf16[16,2048,256]{2,1,0:T(8,128)(2,1)} broadcast(bf16[]{:T(256)} %constant.74.clone.1), dimensions={} | broadcast | bytes 16777218 | tf_op jit(solution)/shard_map/broadcast_in_dim | solution.py:97
  28.1 21.8 %scatter_fusion = bf16[16,2048,256]{2,1,0:T(8,128)(2,1)} fusion(bf16[16,2048,256]{2,1,0:T(8,128)(2,1)} %broadcast.181, s32[8]{0:T(128)S(1)} %get-tuple-element.174, bf16[8,2048,256]{2,1,0:T(8,128)(2,1)} %bitcast.163), kind=kCustom, calls=%fused_computation.4 | custom fusion | bytes 25165856 | tf_op jit(solution)/shard_map/scatter | solution.py:99
  50.0 7.6 %all-to-all-start = ((bf16[16,2048,1,256]{3,1,2,0:T(8,128)(2,1)}), bf16[16,2048,1,256]{3,1,2,0:T(8,128)(2,1)}, u32[]{:S(2)}, u32[]{:S(2)}) async-start(bf16[16,2048,1,256]{3,1,2,0:T(8,128)(2,1)} %bitcast.161), calls=%async_computation | async-start | bytes 33554432 | tf_op jit(solution)/shard_map/all_to_all | solution.py:101
  57.8 0.6 pad_clamp_fusion
  58.5 1.9 multiply_cosine_fusion
  60.5 289.6 %all-to-all-done = bf16[16,2048,1,256]{3,1,2,0:T(8,128)(2,1)} async-done(((bf16[16,2048,1,256]{3,1,2,0:T(8,128)(2,1)}), bf16[16,2048,1,256]{3,1,2,0:T(8,128)(2,1)}, u32[]{:S(2)}, u32[]{:S(2)}) %all-to-all-start) | async-done | bytes 16777248 | tf_op jit(solution)/shard_map/all_to_all | solution.py:101
  350.1 10.4 %gather_fusion.2 = bf16[8,2048,256]{2,1,0:T(8,128)(2,1)} fusion(bf16[16,2048,256]{2,1,0:T(8,128)(2,1)} %bitcast.40, s32[1024]{0:T(1024)S(1)} %pad_clamp_fusion.1), kind=kCustom, calls=%fused_computation.2 | custom fusion | bytes 16777248 | tf_op jit(solution)/shard_map/gather | solution.py:103
  360.5 5.8 %slice_bitcast_fusion = (bf16[8,2048,1,128]{3,1,2,0:T(8,128)(2,1)}, bf16[8,2048,1,128]{3,1,0,2:T(8,128)(2,1)}) fusion(bf16[8,2048,1,256]{3,1,0,2:T(8,128)(2,1)} %bitcast.162), kind=kLoop, calls=%fused_computation.47 | loop fusion | bytes 16777216 | tf_op jit(solution)/shard_map/while | solution.py:45
  366.3 15.7 %fusion.57 = f32[1024,512]{1,0:T(8,128)} fusion(bf16[1024,8192]{1,0:T(8,128)(2,1)} %all-gather.2.cloned.1.call-done, bf16[8192,512]{1,0:T(8,128)(2,1)} %param.12), kind=kOutput, calls=%fused_computation.98 | convolution fusion | flops 8589934592 | bytes 27262976 | tf_op jit(solution)/shard_map/dot_general | solution.py:65
  382.0 1.9 reshape.283
  383.9 1.2 fusion.55
  385.1 0.7 fusion.36
  386.4 4.6 broadcast_in_dim.94
  391.2 42.2 %while.29 = (s32[]{:T(128)}, f32[8,128,1,4,128]{1,4,3,2,0:T(8,128)S(1)}, f32[8,128,1,4]{1,3,2,0:T(4,128)S(1)}, f32[8,128,1,4]{1,3,2,0:T(4,128)S(1)}, bf16[8,2048...) while((s32[]{:T(128)}, ...), condition=%wide.region_9.10_spmd, body=%wide.region_6.9_spmd.sunk | while | flops 544209920 | bytes 14829677 | solution.py:45
  391.2 1.0 dynamic-slice_bitcast_fusion.5
  392.2 1.8 fusion.79
  394.0 1.9 fusion.80
  396.5 1.0 dynamic-slice_bitcast_fusion.5
  397.5 1.8 fusion.79
  399.3 1.9 fusion.80
  401.8 1.0 dynamic-slice_bitcast_fusion.5
  402.8 1.8 fusion.79
  404.5 1.9 fusion.80
  407.1 1.0 dynamic-slice_bitcast_fusion.5
  408.0 1.8 fusion.79
  409.8 1.9 fusion.80
  412.3 1.0 dynamic-slice_bitcast_fusion.5
  413.3 1.8 fusion.79
  415.1 1.9 fusion.80
  417.6 1.0 dynamic-slice_bitcast_fusion.5
  418.6 1.8 fusion.79
  420.4 1.9 fusion.80
  422.9 1.0 dynamic-slice_bitcast_fusion.5
  423.9 1.8 fusion.79
  425.6 1.9 fusion.80
  428.2 1.0 dynamic-slice_bitcast_fusion.5
  429.1 1.8 fusion.79
  430.9 1.9 fusion.80
  433.4 10.0 %fusion.56 = f32[1024,256]{1,0:T(8,128)S(1)} fusion(bf16[1024,8192]{1,0:T(8,128)(2,1)} %all-gather.2.cloned.1.call-done, bf16[8192,256]{1,0:T(8,128)(2,1)} %param.13), kind=kOutput, calls=%fused_computation.97 | convolution fusion | flops 4294967296 | bytes 22020096 | tf_op jit(solution)/shard_map/dot_general | solution.py:66
  443.5 1.0 copy-done.1
  444.7 3.8 fusion.43
  448.5 0.9 pad_maximum_fusion.2
  449.9 1.1 broadcast_in_dim.95
  451.0 2.5 scatter_fusion.1
  453.5 11.1 %all-to-all-start.1 = ((bf16[16,128,256]{2,1,0:T(8,128)(2,1)}), bf16[16,128,256]{2,1,0:T(8,128)(2,1)}, u32[]{:S(2)}, u32[]{:S(2)}) async-start(bf16[16,128,256]{2,1,0:T(8,128)(2,1)} %scatter_fusion.1), calls=%async_computation.1 | async-start | bytes 2097152 | tf_op jit(solution)/shard_map/all_to_all | solution.py:102
  464.9 0.6 broadcast.172.clone.3
  465.5 14.6 %while.28 = (s32[]{:T(128)}, f32[8,128,1,4,128]{1,4,3,2,0:T(8,128)S(1)}, f32[8,128,1,4]{1,3,2,0:T(4,128)S(1)}, f32[8,128,1,4]{1,3,2,0:T(4,128)}, bf16[8,128,1,12...) while((s32[]{:T(128)}, ...), condition=%wide.region_3.4_spmd, body=%wide.region_0.3_spmd.sunk | while | flops 34012160 | bytes 1312877 | solution.py:45
  465.5 1.0 fusion.74
  467.3 1.0 fusion.74
  469.2 1.0 fusion.74
  471.0 1.0 fusion.74
  472.8 1.0 fusion.74
  474.7 1.0 fusion.74
  476.5 1.0 fusion.74
  478.3 1.0 fusion.74
  480.1 0.8 fusion.49
  480.9 2.3 divide_convert_fusion
  483.2 0.7 copy.47
  483.9 1.2 copy.71
  485.1 2.7 gather_fusion.3
  (90 shorter events, 14.4 us)
Async XLA Ops:
  7.2 359.1 %all-gather.2.cloned.1.call-start = ((), (), s32[]{:S(2)}) async-start(), calls=%async_computation.2 | async-start | bytes 18874368 | tf_op jit(solution)/shard_map/all_gather | solution.py:64
  50.0 7.6 %copy-start.4 = (s32[128]{0:T(128)S(1)}, s32[128]{0:T(128)}, u32[]{:S(2)}) copy-start(s32[128]{0:T(128)} %param.15) | copy-start | bytes 1540
  50.0 7.7 %copy-start.5 = (s32[128]{0:T(128)S(1)}, s32[128]{0:T(128)}, u32[]{:S(2)}) copy-start(s32[128]{0:T(128)} %param.16) | copy-start | bytes 1540
  50.0 300.1 %all-to-all-start = ((bf16[16,2048,1,256]{3,1,2,0:T(8,128)(2,1)}), bf16[16,2048,1,256]{3,1,2,0:T(8,128)(2,1)}, u32[]{:S(2)}, u32[]{:S(2)}) async-start(bf16[16,2048,1,256]{3,1,2,0:T(8,128)(2,1)} %bitcast.161), calls=%async_computation | async-start | bytes 33554432 | tf_op jit(solution)/shard_map/all_to_all | solution.py:101
  433.4 10.1 %copy-start = (f32[8,128,1,4,128]{1,4,3,2,0:T(8,128)}, f32[8,128,1,4,128]{1,4,3,2,0:T(8,128)S(1)}, u32[]{:S(2)}) copy-start(f32[8,128,1,4,128]{1,4,3,2,0:T(8,128)S(1)} %get-tuple-element.93) | copy-start | bytes 6291460
  433.4 10.1 %copy-start.2 = (f32[8,128,1,4]{1,3,2,0:T(4,128)}, f32[8,128,1,4]{1,3,2,0:T(4,128)S(1)}, u32[]{:S(2)}) copy-start(f32[8,128,1,4]{1,3,2,0:T(4,128)S(1)} %get-tuple-element.92) | copy-start | bytes 49156
  433.4 10.1 %copy-start.3 = (f32[8,128,1,4]{1,3,2,0:T(4,128)}, f32[8,128,1,4]{1,3,2,0:T(4,128)S(1)}, u32[]{:S(2)}) copy-start(f32[8,128,1,4]{1,3,2,0:T(4,128)S(1)} %get-tuple-element.95) | copy-start | bytes 49156
  443.5 1.0 copy-start.1
  453.5 31.6 %all-to-all-start.1 = ((bf16[16,128,256]{2,1,0:T(8,128)(2,1)}), bf16[16,128,256]{2,1,0:T(8,128)(2,1)}, u32[]{:S(2)}, u32[]{:S(2)}) async-start(bf16[16,128,256]{2,1,0:T(8,128)(2,1)} %scatter_fusion.1), calls=%async_computation.1 | async-start | bytes 2097152 | tf_op jit(solution)/shard_map/all_to_all | solution.py:102
Sparse Core Ops, SparseCore 0:
  9.7 87.3 all-gather.1
where the time goes:
time: 499 us; the launch traced here: 495 us
  waiting for transfers between devices  290 us (58%)
  local copies, waits for them, and re-layouts  88.9 us (18%)
  matrix products  64.6 us (13%)
  starting transfers between devices  18.8 us (4%)
  other arithmetic  17.4 us (3%)
  between operations  14.3 us (3%)
    all_to_all x1, waiting for transfers between devices, body(): lax.all_to_all(prefix_send, 'rep', split_axis=0, concat_axis=0, tiled=True)  290 us
    dot_general x16, matrix products, attend_one(): jnp.einsum('ckgd,skd->ckgs', queries, keys, preferred_element_type=jnp.fl...  21.9 us
    scatter x1, local copies, waits for them, and re-layouts, body(): prefix_send = jnp.zeros((replicas, prefix_span, kv_local, 2 * HEAD_DIM),...  21.8 us
    dot_general x16, matrix products, attend_one(): jnp.einsum('ckgs,skd->ckgd', weights.astype(jnp.bfloat16), values, prefer...  16.9 us
    dot_general x1, matrix products, body(): query = jnp.dot(piece, w_query, preferred_element_type=jnp.float32)  15.7 us
    all_to_all x1, starting transfers between devices, body(): lax.all_to_all(fresh_send, 'rep', split_axis=0, concat_axis=0, tiled=True)  11.1 us
    gather x1, local copies, waits for them, and re-layouts, body(): prefix_mine = prefix_recv[targets]  10.4 us
    dot_general x1, matrix products, body(): keyval = jnp.dot(piece, w_keyval, preferred_element_type=jnp.float32)  10 us
  transfers between devices with their start and end apart: 3, of which 1 were waited for; matrix products, arithmetic and copies ran while one was open for 16% of the time, Pallas kernels for 0%

commit v1 on v0

v1 whole, which is shorter than its diff:
```python
import math

import jax
import jax.numpy as jnp
import numpy as np
from jax import lax
from jax.experimental import pallas as pl
from jax.experimental.pallas import tpu as pltpu
from jax.sharding import PartitionSpec as P

HEAD_DIM = 128
SPAN_LEN = 128
ROPE_BASE = 500000.0
MESH = pl.DeviceIdType.MESH
BF = jnp.bfloat16
F32 = jnp.float32

REPS = 16
STEPS = 8
PAGES = 16
GROUP = 4
ROWS = GROUP * SPAN_LEN
MSG = ROWS + 2 * SPAN_LEN
PIECE = MSG // REPS
BACK = ROWS // REPS
KEYS = PAGES * 128 + SPAN_LEN
CHUNK = 1024
NEAR = 6 * CHUNK
SCALE = 1.0 / math.sqrt(HEAD_DIM)
LOG2E = math.log2(math.e)

T_LEN = SPAN_LEN * PAGES
T_OWN = T_LEN + 128
T_INV = T_OWN + 128


def kernel(
    table, hid, wq_h, wkv_h, pool_h, trig, out, cache,
    gath, wq, wkv, pool, accq, acck, msg, r1, st2, r2, om, r3, st4, r4, scores, work1, work3,
    local_sem, y_send, y_recv, x_send, x_recv,
):
    me = lax.axis_index("rep")
    tp = lax.axis_index("tp")
    y, c = tp // 2, lax.rem(tp, 2)
    up = (me, lax.rem(y + 1, 4) * 2 + c)
    down = (me, lax.rem(y + 3, 4) * 2 + c)
    sib = (me, y * 2 + 1 - c)

    loads = []
    for slot, (rel, other) in enumerate(
        [(0, 0), (0, 1), (3, 0), (1, 0), (3, 1), (1, 1), (2, 0), (2, 1)]
    ):
        core = c if other == 0 else 1 - c
        rows = pl.ds(pl.multiple_of((lax.rem(y + rel, 4) * 2 + core) * CHUNK, CHUNK), CHUNK)
        place = pl.ds(slot * CHUNK, CHUNK)
        loads.append(pltpu.make_async_copy(wq_h.at[rows], wq.at[place], local_sem.at[2 * slot]))
        loads.append(
            pltpu.make_async_copy(wkv_h.at[rows], wkv.at[place], local_sem.at[2 * slot + 1])
        )
    for s in range(STEPS):
        loads.append(
            pltpu.make_async_copy(
                hid.at[pl.ds(s * SPAN_LEN, SPAN_LEN)],
                gath.at[s, :, pl.ds(0, CHUNK)],
                local_sem.at[16 + s],
            )
        )
    loads.append(pltpu.make_async_copy(pool_h, pool, local_sem.at[24]))
    for load in loads:
        load.start()

    barrier = pltpu.get_barrier_semaphore()
    for device in (up, down, sib):
        pl.semaphore_signal(barrier, inc=1, device_id=device, device_id_type=MESH)
    for d in range(1, REPS):
        pl.semaphore_signal(
            barrier, inc=1, device_id=(lax.rem(me + d, REPS), tp), device_id_type=MESH
        )
    pl.semaphore_wait(barrier, 3 + REPS - 1)

    def remote(src, dst, send, recv, device):
        return pltpu.make_async_remote_copy(
            src_ref=src, dst_ref=dst, send_sem=send, recv_sem=recv,
            device_id=device, device_id_type=MESH,
        )

    def part(s, slot, first=0, count=SPAN_LEN):
        return gath.at[s, pl.ds(first, count), pl.ds(slot * CHUNK, CHUNK)]

    half = SPAN_LEN // 2

    def y_copy(kind, s):
        own = hid.at[pl.ds(pl.multiple_of(s * SPAN_LEN, SPAN_LEN), SPAN_LEN)]
        sems = (y_send.at[kind, s], y_recv.at[kind, s])
        if kind == 0:
            return remote(own, part(s, 2), *sems, up)
        if kind == 1:
            return remote(own, part(s, 3), *sems, down)
        if kind == 2:
            return remote(own, part(s, 1), *sems, sib)
        if kind == 3:
            return remote(part(s, 2, 0, half), part(s, 6, 0, half), *sems, up)
        if kind == 4:
            return remote(part(s, 3, half, half), part(s, 6, half, half), *sems, down)
        if kind == 5:
            return remote(part(s, 2), part(s, 4), *sems, sib)
        if kind == 6:
            return remote(part(s, 3), part(s, 5), *sems, sib)
        return remote(part(s, 6), part(s, 7), *sems, sib)

    def near_send(s):
        for kind in (0, 1, 2):
            y_copy(kind, s).start()

    def exchange(phase, s, src, dst):
        def one(d, carry):
            target = lax.rem(me + d, REPS)
            remote(
                src.at[s, target], dst.at[s, me], x_send.at[phase, s], x_recv.at[phase, s],
                (target, tp),
            ).start()
            return carry

        lax.fori_loop(1, REPS, one, 0, unroll=True)
        dst[s, me] = src[s, me]

    def landed(phase, s, dst):
        ref = dst.at[s, pl.ds(0, REPS - 1)]
        pltpu.make_async_copy(ref, ref, x_recv.at[phase, s]).wait()

    def sent(phase, s, src):
        ref = src.at[s, pl.ds(0, REPS - 1)]
        pltpu.make_async_copy(ref, ref, x_send.at[phase, s]).wait()

    near_send(0)
    near_send(1)
    for load in loads:
        load.wait()

    lane = lax.broadcasted_iota(jnp.int32, (1, 128), 1)

    def project_near(s):
        slot = lax.rem(s, 2)
        x = gath[s, :, :NEAR]
        accq[slot] = jnp.dot(x, wq[:NEAR], preferred_element_type=F32)
        acck[slot] = jnp.dot(x, wkv[:NEAR], preferred_element_type=F32)

    def project_far(s):
        slot = lax.rem(s, 2)
        x = gath[s, :, NEAR:]
        query = accq[slot] + jnp.dot(x, wq[NEAR:], preferred_element_type=F32)
        keyval = acck[slot] + jnp.dot(x, wkv[NEAR:], preferred_element_type=F32)
        start = table[T_LEN + me * STEPS + s].astype(F32)
        angle = start * trig[2, :8]
        cos_p, sin_p = jnp.cos(angle)[:1], jnp.sin(angle)[:1]
        cos_t, sin_t = trig[0], trig[1]
        cosine = cos_p * cos_t - sin_p * sin_t
        sine = sin_p * cos_t + cos_p * sin_t
        sine = jnp.where(lane < HEAD_DIM // 2, -sine, sine)

        def rotate(v):
            return (v * cosine + pltpu.roll(v, HEAD_DIM // 2, 1) * sine).astype(BF)

        blocks = [rotate(query[:, h * 128 : (h + 1) * 128]) for h in range(GROUP)]
        blocks.append(rotate(keyval[:, :128]))
        blocks.append(keyval[:, 128:].astype(BF))
        msg[s] = jnp.concatenate(blocks, axis=0).reshape(REPS, PIECE, 128)

    def attend(s):
        row = table[T_INV + s * REPS + me] * STEPS + s
        length = table[T_LEN + row]
        whole = r2[s].reshape(MSG, 128)
        q = whole[:ROWS]
        fresh_k, fresh_v = whole[ROWS : ROWS + 128], whole[ROWS + 128 :]
        cache[s, :, :128] = fresh_k
        cache[s, :, 128:] = fresh_v
        nt = (((1,), (1,)), ((), ()))

        def page(j):
            return pool[table[row * PAGES + j]]

        t = lax.rem(lax.broadcasted_iota(jnp.int32, (ROWS, 128), 0), SPAN_LEN)
        t_key = lax.broadcasted_iota(jnp.int32, (ROWS, 128), 1)
        sc = lax.dot_general(q, fresh_k, nt, preferred_element_type=F32)
        sc = jnp.where(t_key <= t, sc, -jnp.inf)
        scores[:, PAGES * 128 :] = sc
        top = sc
        position = lax.broadcasted_iota(jnp.int32, (1, 256), 1)
        for j in range(0, PAGES, 2):
            keys = jnp.concatenate([page(j)[:, :128], page(j + 1)[:, :128]], axis=0)
            bias = jnp.where(position + j * 128 < length, 0.0, -jnp.inf)
            sc = lax.dot_general(q, keys, nt, preferred_element_type=F32) + bias
            scores[:, j * 128 : (j + 2) * 128] = sc
            top = jnp.maximum(top, jnp.maximum(sc[:, :128], sc[:, 128:]))
        factor = SCALE * LOG2E
        highest = jnp.max(top, axis=1, keepdims=True) * factor
        w = jnp.exp2(scores[:, PAGES * 128 :] * factor - highest)
        total = w
        summed = jnp.dot(w.astype(BF), fresh_v, preferred_element_type=F32)
        for j in range(0, PAGES, 2):
            values = jnp.concatenate([page(j)[:, 128:], page(j + 1)[:, 128:]], axis=0)
            w = jnp.exp2(scores[:, j * 128 : (j + 2) * 128] * factor - highest)
            total = total + (w[:, :128] + w[:, 128:])
            summed = summed + jnp.dot(w.astype(BF), values, preferred_element_type=F32)
        total = jnp.sum(total, axis=1, keepdims=True)
        om[s] = (summed / total).astype(BF).reshape(REPS, BACK, 128)

    def when(s):
        return pl.when((s >= 0) & (s < STEPS))

    def step(it, carry):
        @when(it + 2)
        def _():
            near_send(it + 2)

        @when(it)
        def _():
            y_copy(0, it).wait_recv()
            y_copy(3, it).start()
            y_copy(5, it).start()
            y_copy(1, it).wait_recv()
            y_copy(4, it).start()
            y_copy(6, it).start()

        @when(it - 1)
        def _():
            y_copy(3, it - 1).wait_recv()
            y_copy(4, it - 1).wait_recv()
            y_copy(7, it - 1).start()

        @when(it - 2)
        def _():
            s = it - 2
            landed(0, s, r1)
            work1[...] = r1[s]
            for o in range(REPS):
                st2[s, o] = work1[table[T_INV + s * REPS + o]]
            exchange(1, s, st2, r2)

        @when(it - 4)
        def _():
            s = it - 4
            landed(2, s, r3)
            work3[...] = r3[s]
            for r in range(REPS):
                st4[s, r] = work3[table[T_OWN + r * STEPS + s]]
            exchange(3, s, st4, r4)

        @when(it)
        def _():
            for kind in (2, 5, 6):
                y_copy(kind, it).wait_recv()
            project_near(it)

        @when(it - 1)
        def _():
            y_copy(7, it - 1).wait_recv()
            project_far(it - 1)
            exchange(0, it - 1, msg, r1)

        @when(it - 3)
        def _():
            landed(1, it - 3, r2)
            attend(it - 3)
            exchange(2, it - 3, om, r3)

        @when(it - 5)
        def _():
            s = it - 5
            landed(3, s, r4)
            rows = pl.ds(pl.multiple_of(s * SPAN_LEN, SPAN_LEN), SPAN_LEN)
            whole = r4[s].reshape(ROWS, 128)
            for h in range(GROUP):
                out[rows, h * 128 : (h + 1) * 128] = whole[h * 128 : (h + 1) * 128]

        return carry

    lax.fori_loop(0, STEPS + 5, step, 0)

    def drain(s, carry):
        for kind in range(8):
            y_copy(kind, s).wait_send()
        sent(0, s, msg)
        sent(1, s, st2)
        sent(2, s, om)
        sent(3, s, st4)
        return carry

    lax.fori_loop(0, STEPS, drain, 0)


def trig_tables():
    i = np.arange(64, dtype=np.float64)
    frequency = np.concatenate([ROPE_BASE ** (-2.0 * i / HEAD_DIM)] * 2)
    angle = np.arange(SPAN_LEN, dtype=np.float64)[:, None] * frequency[None, :]
    wide = np.broadcast_to(frequency[None, :], (SPAN_LEN, HEAD_DIM))
    return np.stack([np.cos(angle), np.sin(angle), wide]).astype(np.float32)


def body(hidden, w_query, w_keyval, kv_pool, prefix_len, owner, block_table):
    by_step = owner.reshape(REPS, STEPS).T
    ids = jnp.arange(REPS, dtype=jnp.int32)
    inverse = jnp.sum(
        jnp.where(by_step[:, None, :] == ids[None, :, None], ids[None, None, :], 0), axis=2
    )
    table = jnp.concatenate(
        [block_table.reshape(-1), prefix_len, owner, inverse.reshape(-1).astype(jnp.int32)]
    )
    v = pltpu.VMEM
    dma = pltpu.SemaphoreType.DMA
    any_spec = pl.BlockSpec(memory_space=pl.ANY)
    vmem = pl.BlockSpec(memory_space=pltpu.VMEM)
    return pl.pallas_call(
        kernel,
        out_shape=(
            jax.ShapeDtypeStruct((STEPS * SPAN_LEN, GROUP * 128), BF),
            jax.ShapeDtypeStruct((STEPS, SPAN_LEN, 256), BF),
        ),
        in_specs=[pl.BlockSpec(memory_space=pltpu.SMEM)] + [any_spec] * 4 + [vmem],
        out_specs=(vmem, vmem),
        scratch_shapes=[
            v((STEPS, SPAN_LEN, 8 * CHUNK), BF),
            v((8 * CHUNK, GROUP * 128), BF),
            v((8 * CHUNK, 256), BF),
            v((128, 128, 256), BF),
            v((2, SPAN_LEN, GROUP * 128), F32),
            v((2, SPAN_LEN, 256), F32),
            v((STEPS, REPS, PIECE, 128), BF),
            v((STEPS, REPS, PIECE, 128), BF),
            v((STEPS, REPS, PIECE, 128), BF),
            v((STEPS, REPS, PIECE, 128), BF),
            v((STEPS, REPS, BACK, 128), BF),
            v((STEPS, REPS, BACK, 128), BF),
            v((STEPS, REPS, BACK, 128), BF),
            v((STEPS, REPS, BACK, 128), BF),
            v((ROWS, KEYS), F32),
            v((REPS, PIECE, 128), BF),
            v((REPS, BACK, 128), BF),
            dma((25,)),
            dma((8, STEPS)),
            dma((8, STEPS)),
            dma((4, STEPS)),
            dma((4, STEPS)),
        ],
        compiler_params=pltpu.CompilerParams(
            collective_id=0, has_side_effects=True, vmem_limit_bytes=62 * 1024 * 1024
        ),
        cost_estimate=pl.CostEstimate(
            flops=18_000_000_000, bytes_accessed=24_000_000, transcendentals=9_000_000
        ),
    )(table, hidden, w_query, w_keyval, kv_pool, jnp.asarray(trig_tables()))


def solution(mesh):
    placed = (P("rep", "tp"), P(None, "tp"), P(None, "tp"), P("rep", None, "tp"), P(), P(), P())
    return jax.shard_map(
        body,
        mesh=mesh,
        in_specs=placed,
        out_specs=(P("rep", "tp"), P("rep", None, "tp")),
        check_vma=False,
    )
```

time: 499 us -> 145 us (0.29)
  waiting for transfers between devices: 290 us -> 0 us
  Pallas kernels: 0 us -> 137 us
  local copies, waits for them, and re-layouts: 88.9 us -> 5.9 us
  matrix products: 64.6 us -> 0 us
  starting transfers between devices: 18.8 us -> 0 us
  other arithmetic: 17.4 us -> 1.5 us
  between operations: 14.3 us -> 0.64 us
    all_to_all x2 -> x0, waiting for transfers between devices: 290 us -> none  [the longest x1 290 us: body(): lax.all_to_all(prefix_send, 'rep', split_axis=0, concat_axis=0, tiled=True)]
    pallas_call x0 -> x1, Pallas kernels: none -> 137 us  [body(): pl.pallas_call(kernel, out_shape=(jax.ShapeDtypeStruct((STEPS * SPAN_LEN,...]
    dot_general x34 -> x0, matrix products: 64.6 us -> none  [the longest x16 21.9 us: attend_one(): jnp.einsum('ckgd,skd->ckgs', queries, keys, preferred_element_type=jnp.fl...]
    scatter x2 -> x0, local copies, waits for them, and re-layouts: 24.3 us -> none  [the longest x1 21.8 us: body(): prefix_send = jnp.zeros((replicas, prefix_span, kv_local, 2 * HEAD_DIM),...]
    gather x4 -> x0, local copies, waits for them, and re-layouts: 23.7 us -> none  [the longest x1 10.4 us: body(): prefix_mine = prefix_recv[targets]]
    broadcast_in_dim x20 -> x0, local copies, waits for them, and re-layouts: 21.5 us -> none  [the longest x1 7.98 us: body(): jnp.zeros((replicas, prefix_span, kv_local, 2 * HEAD_DIM), jnp.bfloat16)]
    all_to_all x2 -> x0, starting transfers between devices: 18.7 us -> none  [the longest x1 11.1 us: body(): lax.all_to_all(fresh_send, 'rep', split_axis=0, concat_axis=0, tiled=True)]
    while x1 -> x0, local copies, waits for them, and re-layouts: 5.77 us -> none  [attend_part(): lax.map(lambda items: attend_one(items[0], items[1], items[2], items[3]),...]
  transfers between devices with their start and end apart: 3 -> 0, of which waited for: 1 -> 0; matrix products, arithmetic and copies ran while one was open for 16% -> 0% of each run, Pallas kernels for 0% -> 0%
where the time goes in v1:
time: 145 us
  Pallas kernels  137 us (94%)
  local copies, waits for them, and re-layouts  5.9 us (4%)
  other arithmetic  1.5 us (1%)
    pallas_call x1, Pallas kernels, body(): pl.pallas_call(kernel, out_shape=(jax.ShapeDtypeStruct((STEPS * SPAN_LEN,...  137 us
    unnamed x3, local copies, waits for them, and re-layouts  4.94 us

profile of v1, /device:TPU:0, one launch (start us, length us, event | category | flops | bytes accessed | tf_op | source)
XLA Modules:
  0.0 144.7 jit_solution(3481343963400232952)
XLA Ops:
  0.6 0.7 reshape.15
  1.4 0.1 copy.14
  1.4 0.2 select_reduce_fusion
  1.7 0.1 reshape.16
  1.7 0.8 copy.13
  2.5 0.1 reshape.14
  2.6 1.3 pad_add_fusion.table
  3.9 136.7 %shard_map.95 = (bf16[1024,512]{1,0:T(8,128)(2,1)}, bf16[8,128,256]{2,1,0:T(8,128)(2,1)}) custom-call(s32[2432]{0:T(1024)} %pad_add_fusion.table, bf16[1024,1024]{1,0:T(8,128)(2,1)} %hid.1, bf16[8192,512]{1,0:T(8,128)(2,1)} %wq_h.1, bf16[8192,256]{1,0:T(8,128)(2,1)} %wkv_h.1, bf16[128,128,256]{2,1,0:T(8,128)(2,1)} %pool_h.1, f32[3,128,128]{2,1,0:T(8,128)} %constant.4.clone.trig), custom_call_target="tpu_custom_call" | custom-call | flops 17999998976 | bytes 24000000 | tf_op jit(solution)/shard_map/pallas_call | solution.py:313
  140.6 2.3 %copy.17 = bf16[1024,512]{1,0:T(8,128)(2,1)} copy(bf16[1024,512]{1,0:T(8,128)(2,1)} %get-tuple-element.4) | data formatting | bytes 2097152
  142.9 1.9 %copy.18 = bf16[8,128,256]{2,1,0:T(8,128)(2,1)} copy(bf16[8,128,256]{2,1,0:T(8,128)(2,1)} %get-tuple-element.5) | data formatting | bytes 1048576

commit v2 on v1

v2 whole, which is shorter than its diff:
```python
import math

import jax
import jax.numpy as jnp
import numpy as np
from jax import lax
from jax.experimental import pallas as pl
from jax.experimental.pallas import tpu as pltpu
from jax.sharding import PartitionSpec as P

HEAD_DIM = 128
SPAN_LEN = 128
ROPE_BASE = 500000.0
MESH = pl.DeviceIdType.MESH
BF = jnp.bfloat16
F32 = jnp.float32

REPS = 16
STEPS = 8
PAGES = 16
GROUP = 4
ROWS = GROUP * SPAN_LEN
MSG = ROWS + 2 * SPAN_LEN
PIECE = MSG // REPS
BACK = ROWS // REPS
KEYS = PAGES * 128 + SPAN_LEN
CHUNK = 1024
NEAR = 6 * CHUNK
SCALE = 1.0 / math.sqrt(HEAD_DIM)
LOG2E = math.log2(math.e)

EARLY = 2
LATE = STEPS - EARLY
HALF = CHUNK // 2
BLOCK = 256
OFFSETS = [
    (2, 2), (2, 1), (1, 2), (2, 3), (3, 2), (1, 1), (3, 3), (1, 3), (3, 1),
    (0, 2), (2, 0), (0, 1), (1, 0), (0, 3), (3, 0),
]


def kernel(
    lens, owner, pages, hid, wq_h, wkv_h, pool_h, trig, out, cache,
    gath, wq, wkv, pool, accq, acck, hv, rh, sth, msg, r1, st2, r2, om, r3, st4, r4,
    scores, workh, work1, work3,
    local_sem, y_send, y_recv, x_send, x_recv,
):
    me = lax.axis_index("rep")
    tp = lax.axis_index("tp")
    y, c = tp // 2, lax.rem(tp, 2)
    up = (me, lax.rem(y + 1, 4) * 2 + c)
    down = (me, lax.rem(y + 3, 4) * 2 + c)
    sib = (me, y * 2 + 1 - c)
    peers = [
        lax.rem(me // 4 + dx, 4) * 4 + lax.rem(lax.rem(me, 4) + dz, 4) for dx, dz in OFFSETS
    ]

    loads = []

    def load(src, dst):
        loads.append(pltpu.make_async_copy(src, dst, local_sem.at[len(loads)]))

    for s in range(EARLY):
        load(hid.at[pl.ds(s * SPAN_LEN, SPAN_LEN)], gath.at[s, :, pl.ds(0, CHUNK)])
    for s in range(LATE):
        for h in range(2):
            load(
                hid.at[pl.ds((EARLY + s) * SPAN_LEN, SPAN_LEN), pl.ds(h * HALF, HALF)],
                hv.at[s, h],
            )
    hidden_loads = len(loads)
    for slot, (rel, other) in enumerate(
        [(0, 0), (0, 1), (3, 0), (1, 0), (3, 1), (1, 1), (2, 0), (2, 1)]
    ):
        core = c if other == 0 else 1 - c
        rows = pl.ds(pl.multiple_of((lax.rem(y + rel, 4) * 2 + core) * CHUNK, CHUNK), CHUNK)
        place = pl.ds(slot * CHUNK, CHUNK)
        load(wq_h.at[rows], wq.at[place])
        load(wkv_h.at[rows], wkv.at[place])
    load(pool_h, pool)
    for one in loads:
        one.start()

    barrier = pltpu.get_barrier_semaphore()
    for device in (up, down, sib):
        pl.semaphore_signal(barrier, inc=1, device_id=device, device_id_type=MESH)
    for peer in peers:
        pl.semaphore_signal(barrier, inc=1, device_id=(peer, tp), device_id_type=MESH)
    for one in loads[:hidden_loads]:
        one.wait()
    pl.semaphore_wait(barrier, 3 + REPS - 1)

    def remote(src, dst, send, recv, device):
        return pltpu.make_async_remote_copy(
            src_ref=src, dst_ref=dst, send_sem=send, recv_sem=recv,
            device_id=device, device_id_type=MESH,
        )

    def part(s, slot, first=0, count=SPAN_LEN):
        return gath.at[s, pl.ds(first, count), pl.ds(slot * CHUNK, CHUNK)]

    half = SPAN_LEN // 2

    def y_copy(kind, s):
        sems = (y_send.at[kind, s], y_recv.at[kind, s])
        if kind == 0:
            return remote(part(s, 0), part(s, 2), *sems, up)
        if kind == 1:
            return remote(part(s, 0), part(s, 3), *sems, down)
        if kind == 2:
            return remote(part(s, 0), part(s, 1), *sems, sib)
        if kind == 3:
            return remote(part(s, 2, 0, half), part(s, 6, 0, half), *sems, up)
        if kind == 4:
            return remote(part(s, 3, half, half), part(s, 6, half, half), *sems, down)
        if kind == 5:
            return remote(part(s, 2), part(s, 4), *sems, sib)
        if kind == 6:
            return remote(part(s, 3), part(s, 5), *sems, sib)
        return remote(part(s, 6), part(s, 7), *sems, sib)

    def near_send(s):
        for kind in (0, 1, 2):
            y_copy(kind, s).start()

    def exchange(phase, s, src, dst):
        for peer in peers:
            remote(
                src(peer), dst, x_send.at[phase, s], x_recv.at[phase, s], (peer, tp)
            ).start()

    def arrived(sem, ref):
        ref = ref.at[0, pl.ds(0, REPS - 1)]
        pltpu.make_async_copy(ref, ref, sem).wait()

    def sources(s):
        owners = [owner[r * STEPS + s] for r in range(REPS)]

        def of(o):
            found = jnp.int32(0)
            for r in range(1, REPS):
                found = jnp.where(owners[r] == o, r, found)
            return found

        return of

    def hidden_out(s):
        u = s - EARLY

        def src(j):
            return hv.at[u, j // 8, pl.ds(pl.multiple_of(lax.rem(j, 8) * 16, 16), 16)]

        exchange(4, s, src, rh.at[u, me])
        rh[u, me] = hv[u, me // 8, pl.ds(pl.multiple_of(lax.rem(me, 8) * 16, 16), 16)]

    def hidden_on(s):
        u = s - EARLY
        arrived(x_recv.at[4, s], rh)
        workh[...] = rh[u]
        of = sources(s)
        for o in range(REPS):
            sth[u, o] = workh[of(o)]
        rows = pl.ds(pl.multiple_of(lax.rem(me, 8) * 16, 16), 16)
        cols = pl.ds(pl.multiple_of(me // 8 * HALF, HALF), HALF)
        exchange(5, s, lambda o: sth.at[u, o], gath.at[s, rows, cols])
        for h in range(2):

            @pl.when(me // 8 == h)
            def _():
                gath[s, rows, h * HALF : (h + 1) * HALF] = sth[u, me]

    near_send(0)
    near_send(1)
    lax.fori_loop(EARLY, 2 * EARLY, lambda s, _: hidden_out(s), None)
    lax.fori_loop(EARLY, 2 * EARLY, lambda s, _: hidden_on(s), None)
    lax.fori_loop(2 * EARLY, 3 * EARLY, lambda s, _: hidden_out(s), None)
    for one in loads[hidden_loads:]:
        one.wait()

    lane = lax.broadcasted_iota(jnp.int32, (1, 128), 1)

    def project_near(s):
        slot = lax.rem(s, 2)
        x = gath[s, :, :NEAR]
        accq[slot] = jnp.dot(x, wq[:NEAR], preferred_element_type=F32)
        acck[slot] = jnp.dot(x, wkv[:NEAR], preferred_element_type=F32)

    def owned(s):
        return sources(s)(me) * STEPS + s

    def project_far(s):
        slot = lax.rem(s, 2)
        x = gath[s, :, NEAR:]
        query = accq[slot] + jnp.dot(x, wq[NEAR:], preferred_element_type=F32)
        keyval = acck[slot] + jnp.dot(x, wkv[NEAR:], preferred_element_type=F32)
        span = jnp.where(s < EARLY, me * STEPS + s, owned(s))
        angle = lens[span].astype(F32) * trig[2, :8]
        cos_p, sin_p = jnp.cos(angle)[:1], jnp.sin(angle)[:1]
        cos_t, sin_t = trig[0], trig[1]
        cosine = cos_p * cos_t - sin_p * sin_t
        sine = sin_p * cos_t + cos_p * sin_t
        sine = jnp.where(lane < HEAD_DIM // 2, -sine, sine)

        def rotate(v):
            return (v * cosine + pltpu.roll(v, HEAD_DIM // 2, 1) * sine).astype(BF)

        blocks = [rotate(query[:, h * 128 : (h + 1) * 128]) for h in range(GROUP)]
        blocks.append(rotate(keyval[:, :128]))
        blocks.append(keyval[:, 128:].astype(BF))
        return jnp.concatenate(blocks, axis=0).reshape(REPS, PIECE, 128)

    def attend(s):
        row = owned(s)
        length = lens[row]
        whole = r2[s].reshape(MSG, 128)
        fresh_k, fresh_v = whole[ROWS : ROWS + 128], whole[ROWS + 128 :]
        cache[s, :, :128] = fresh_k
        cache[s, :, 128:] = fresh_v
        nt = (((1,), (1,)), ((), ()))

        def page(j):
            return pool[pages[j, row]]

        position = lax.broadcasted_iota(jnp.int32, (1, 256), 1)
        t_key = lax.broadcasted_iota(jnp.int32, (BLOCK, 128), 1)
        t = lax.rem(lax.broadcasted_iota(jnp.int32, (BLOCK, 128), 0), SPAN_LEN)
        factor = SCALE * LOG2E
        for first in range(0, ROWS, BLOCK):
            q = whole[first : first + BLOCK]
            sc = lax.dot_general(q, fresh_k, nt, preferred_element_type=F32)
            sc = jnp.where(t_key <= t, sc, -jnp.inf)
            scores[:, PAGES * 128 :] = sc
            top = sc
            for j in range(0, PAGES, 2):
                keys = jnp.concatenate([page(j)[:, :128], page(j + 1)[:, :128]], axis=0)
                bias = jnp.where(position + j * 128 < length, 0.0, -jnp.inf)
                sc = lax.dot_general(q, keys, nt, preferred_element_type=F32) + bias
                scores[:, j * 128 : (j + 2) * 128] = sc
                top = jnp.maximum(top, jnp.maximum(sc[:, :128], sc[:, 128:]))
            highest = jnp.max(top, axis=1, keepdims=True) * factor
            w = jnp.exp2(scores[:, PAGES * 128 :] * factor - highest)
            total = w
            summed = jnp.dot(w.astype(BF), fresh_v, preferred_element_type=F32)
            for j in range(0, PAGES, 2):
                values = jnp.concatenate([page(j)[:, 128:], page(j + 1)[:, 128:]], axis=0)
                w = jnp.exp2(scores[:, j * 128 : (j + 2) * 128] * factor - highest)
                total = total + (w[:, :128] + w[:, 128:])
                summed = summed + jnp.dot(w.astype(BF), values, preferred_element_type=F32)
            total = jnp.sum(total, axis=1, keepdims=True)
            done = (summed / total).astype(BF).reshape(BLOCK // BACK, BACK, 128)
            om[s, first // BACK : (first + BLOCK) // BACK] = done

    def between(s, low, high):
        return pl.when((s >= low) & (s < high))

    def late_and_early(late, early, run):
        def one(n, carry):
            s = jnp.where(n == 0, late, early)

            @between(s, jnp.where(n == 0, EARLY, 0), jnp.where(n == 0, STEPS, EARLY))
            def _():
                run(s)

            return carry

        lax.fori_loop(0, 2, one, 0)

    def back_on(s):
        arrived(x_recv.at[2, s], r3)
        work3[...] = r3[s]
        for r in range(REPS):
            st4[s, r] = work3[owner[r * STEPS + s]]
        exchange(3, s, lambda r: st4.at[s, r], r4.at[s, me])
        r4[s, me] = st4[s, me]

    def finish(s):
        arrived(x_recv.at[3, s], r4)
        rows = pl.ds(pl.multiple_of(s * SPAN_LEN, SPAN_LEN), SPAN_LEN)
        whole = r4[s].reshape(ROWS, 128)
        for h in range(GROUP):
            out[rows, h * 128 : (h + 1) * 128] = whole[h * 128 : (h + 1) * 128]

    def work(s):
        @pl.when(s < EARLY)
        def _():
            arrived(x_recv.at[1, s], r1)

        attend(s)
        exchange(2, s, lambda j: om.at[s, j], r3.at[s, me])
        r3[s, me] = om[s, me]

    def step(it, carry):
        @between(it, 0, STEPS)
        def _():
            y_copy(0, it).wait_recv()
            y_copy(3, it).start()
            y_copy(5, it).start()
            y_copy(1, it).wait_recv()
            y_copy(4, it).start()
            y_copy(6, it).start()

        @between(it - 1, 0, STEPS)
        def _():
            y_copy(3, it - 1).wait_recv()
            y_copy(4, it - 1).wait_recv()
            y_copy(7, it - 1).start()

        late_and_early(it - 2, it - 5, back_on)

        @between(it - 2, 0, EARLY)
        def _():
            s = it - 2
            arrived(x_recv.at[0, s], r1)
            work1[...] = r1[s]
            of = sources(s)
            for o in range(REPS):
                st2[s, o] = work1[of(o)]
            exchange(1, s, lambda o: st2.at[s, o], r2.at[s, me])
            r2[s, me] = st2[s, me]

        @between(it + 4, 2 * EARLY, STEPS)
        def _():
            hidden_on(it + 4)

        @between(it + 6, 3 * EARLY, STEPS)
        def _():
            hidden_out(it + 6)

        @between(it - 1, 0, STEPS)
        def _():
            s = it - 1
            y_copy(7, s).wait_recv()
            whole = project_far(s)

            @pl.when(s < EARLY)
            def _():
                msg[s] = whole
                exchange(0, s, lambda j: msg.at[s, j], r1.at[s, me])
                r1[s, me] = msg[s, me]

            @pl.when(s >= EARLY)
            def _():
                r2[s] = whole

        @between(it + 2, EARLY, STEPS)
        def _():
            arrived(x_recv.at[5, it + 2], rh)
            near_send(it + 2)

        late_and_early(it - 1, it - 4, work)

        @between(it, 0, STEPS)
        def _():
            for kind in (2, 5, 6):
                y_copy(kind, it).wait_recv()
            project_near(it)

        late_and_early(it - 3, it - 6, finish)
        return carry

    lax.fori_loop(0, STEPS + 3, step, 0)

    def drain(s, carry):
        for kind in range(8):
            y_copy(kind, s).wait_send()
        arrived(x_send.at[2, s], om)
        arrived(x_send.at[3, s], st4)

        @pl.when(s < EARLY)
        def _():
            arrived(x_send.at[0, s], msg)
            arrived(x_send.at[1, s], st2)

        @pl.when(s >= EARLY)
        def _():
            arrived(x_send.at[4, s], rh)
            arrived(x_send.at[5, s], sth)

        return carry

    lax.fori_loop(0, STEPS, drain, 0)


def trig_tables():
    i = np.arange(64, dtype=np.float64)
    frequency = np.concatenate([ROPE_BASE ** (-2.0 * i / HEAD_DIM)] * 2)
    angle = np.arange(SPAN_LEN, dtype=np.float64)[:, None] * frequency[None, :]
    wide = np.broadcast_to(frequency[None, :], (SPAN_LEN, HEAD_DIM))
    return np.stack([np.cos(angle), np.sin(angle), wide]).astype(np.float32)


def body(hidden, w_query, w_keyval, kv_pool, prefix_len, owner, block_table):
    v = pltpu.VMEM
    dma = pltpu.SemaphoreType.DMA
    any_spec = pl.BlockSpec(memory_space=pl.ANY)
    vmem = pl.BlockSpec(memory_space=pltpu.VMEM)
    return pl.pallas_call(
        kernel,
        out_shape=(
            jax.ShapeDtypeStruct((STEPS * SPAN_LEN, GROUP * 128), BF),
            jax.ShapeDtypeStruct((STEPS, SPAN_LEN, 256), BF),
        ),
        in_specs=[pl.BlockSpec(memory_space=pltpu.SMEM)] * 3 + [any_spec] * 4 + [vmem],
        out_specs=(vmem, vmem),
        scratch_shapes=[
            v((STEPS, SPAN_LEN, 8 * CHUNK), BF),
            v((8 * CHUNK, GROUP * 128), BF),
            v((8 * CHUNK, 256), BF),
            v((128, 128, 256), BF),
            v((2, SPAN_LEN, GROUP * 128), F32),
            v((2, SPAN_LEN, 256), F32),
            v((LATE, 2, SPAN_LEN, HALF), BF),
            v((LATE, REPS, 16, HALF), BF),
            v((LATE, REPS, 16, HALF), BF),
            v((EARLY, REPS, PIECE, 128), BF),
            v((EARLY, REPS, PIECE, 128), BF),
            v((EARLY, REPS, PIECE, 128), BF),
            v((STEPS, REPS, PIECE, 128), BF),
            v((STEPS, REPS, BACK, 128), BF),
            v((STEPS, REPS, BACK, 128), BF),
            v((STEPS, REPS, BACK, 128), BF),
            v((STEPS, REPS, BACK, 128), BF),
            v((BLOCK, KEYS), F32),
            v((REPS, 16, HALF), BF),
            v((REPS, PIECE, 128), BF),
            v((REPS, BACK, 128), BF),
            dma((31,)),
            dma((8, STEPS)),
            dma((8, STEPS)),
            dma((6, STEPS)),
            dma((6, STEPS)),
        ],
        compiler_params=pltpu.CompilerParams(
            collective_id=0, has_side_effects=True, vmem_limit_bytes=62 * 1024 * 1024
        ),
        cost_estimate=pl.CostEstimate(
            flops=18_000_000_000, bytes_accessed=24_000_000, transcendentals=9_000_000
        ),
    )(prefix_len, owner, block_table.T, hidden, w_query, w_keyval, kv_pool, jnp.asarray(trig_tables()))


def solution(mesh):
    placed = (P("rep", "tp"), P(None, "tp"), P(None, "tp"), P("rep", None, "tp"), P(), P(), P())
    return jax.shard_map(
        body,
        mesh=mesh,
        in_specs=placed,
        out_specs=(P("rep", "tp"), P("rep", None, "tp")),
        check_vma=False,
    )
```

time: 145 us -> 114 us (0.79)
  Pallas kernels: 137 us -> 109 us
  local copies, waits for them, and re-layouts: 5.9 us -> 4.13 us
  other arithmetic: 1.5 us -> 0 us
    pallas_call x1, Pallas kernels: 137 us -> 109 us  [body(): pl.pallas_call(kernel, out_shape=(jax.ShapeDtypeStruct((STEPS * SPAN_LEN,...]
    unnamed x3 -> x2, local copies, waits for them, and re-layouts: 4.94 us -> 4.13 us
where the time goes in v2:
time: 114 us
  Pallas kernels  109 us (96%)
  local copies, waits for them, and re-layouts  4.13 us (4%)
    pallas_call x1, Pallas kernels, body(): pl.pallas_call(kernel, out_shape=(jax.ShapeDtypeStruct((STEPS * SPAN_LEN,...  109 us
    unnamed x2, local copies, waits for them, and re-layouts  4.13 us

profile of v2, /device:TPU:0, one launch (start us, length us, event | category | flops | bytes accessed | tf_op | source)
XLA Modules:
  0.0 114.2 jit_solution(14754091195553172856)
XLA Ops:
  0.6 109.4 %shard_map.95 = (bf16[1024,512]{1,0:T(8,128)(2,1)}, bf16[8,128,256]{2,1,0:T(8,128)(2,1)}) custom-call(s32[128]{0:T(128)} %lens.1, s32[128]{0:T(128)} %owner.1, s32[16,128]{1,0:T(8,128)} %bitcast.1, bf16[1024,1024]{1,0:T(8,128)(2,1)} %hid.1, bf16[8192,512]{1,0:T(8,128)(2,1)} %wq_h.1, bf16[8192,256]{1,0:T(8,128)(2,1)} %wkv_h.1, bf16[128,128,256]{2,1,0:T(8,128)(2,1)} %pool_h.1, ...), custom_call_target="tpu_custom_call" | custom-call | flops 17999998976 | bytes 24000000 | tf_op jit(solution)/shard_map/pallas_call | solution.py:397
  110.1 2.3 %copy.12 = bf16[1024,512]{1,0:T(8,128)(2,1)} copy(bf16[1024,512]{1,0:T(8,128)(2,1)} %get-tuple-element.4) | data formatting | bytes 2097152
  112.3 1.9 %copy.13 = bf16[8,128,256]{2,1,0:T(8,128)(2,1)} copy(bf16[8,128,256]{2,1,0:T(8,128)(2,1)} %get-tuple-element.5) | data formatting | bytes 1048576

commit v3 on v2

--- a/solution.py
+++ b/solution.py
@@ -29,7 +29,7 @@
 SCALE = 1.0 / math.sqrt(HEAD_DIM)
 LOG2E = math.log2(math.e)
 
-EARLY = 2
+EARLY = 3
 LATE = STEPS - EARLY
 HALF = CHUNK // 2
 BLOCK = 256
@@ -42,8 +42,8 @@
 def kernel(
     lens, owner, pages, hid, wq_h, wkv_h, pool_h, trig, out, cache,
     gath, wq, wkv, pool, accq, acck, hv, rh, sth, msg, r1, st2, r2, om, r3, st4, r4,
-    scores, workh, work1, work3,
-    local_sem, y_send, y_recv, x_send, x_recv,
+    scores, workh, work1, work3, outv, cachev,
+    local_sem, out_sem, y_send, y_recv, x_send, x_recv,
 ):
     me = lax.axis_index("rep")
     tp = lax.axis_index("tp")
@@ -171,9 +171,7 @@
 
     near_send(0)
     near_send(1)
-    lax.fori_loop(EARLY, 2 * EARLY, lambda s, _: hidden_out(s), None)
-    lax.fori_loop(EARLY, 2 * EARLY, lambda s, _: hidden_on(s), None)
-    lax.fori_loop(2 * EARLY, 3 * EARLY, lambda s, _: hidden_out(s), None)
+    lax.fori_loop(EARLY, EARLY + 2, lambda s, _: hidden_out(s), None)
     for one in loads[hidden_loads:]:
         one.wait()
 
@@ -209,13 +207,21 @@
         blocks.append(keyval[:, 128:].astype(BF))
         return jnp.concatenate(blocks, axis=0).reshape(REPS, PIECE, 128)
 
+    def cache_copy(s):
+        return pltpu.make_async_copy(cachev.at[s], cache.at[s], out_sem.at[0, s])
+
+    def out_copy(s):
+        rows = pl.ds(pl.multiple_of(s * SPAN_LEN, SPAN_LEN), SPAN_LEN)
+        return pltpu.make_async_copy(outv.at[s], out.at[rows], out_sem.at[1, s])
+
     def attend(s):
         row = owned(s)
         length = lens[row]
         whole = r2[s].reshape(MSG, 128)
         fresh_k, fresh_v = whole[ROWS : ROWS + 128], whole[ROWS + 128 :]
-        cache[s, :, :128] = fresh_k
-        cache[s, :, 128:] = fresh_v
+        cachev[s, :, :128] = fresh_k
+        cachev[s, :, 128:] = fresh_v
+        cache_copy(s).start()
         nt = (((1,), (1,)), ((), ()))
 
         def page(j):
@@ -275,10 +281,10 @@
 
     def finish(s):
         arrived(x_recv.at[3, s], r4)
-        rows = pl.ds(pl.multiple_of(s * SPAN_LEN, SPAN_LEN), SPAN_LEN)
         whole = r4[s].reshape(ROWS, 128)
         for h in range(GROUP):
-            out[rows, h * 128 : (h + 1) * 128] = whole[h * 128 : (h + 1) * 128]
+            outv[s, :, h * 128 : (h + 1) * 128] = whole[h * 128 : (h + 1) * 128]
+        out_copy(s).start()
 
     def work(s):
         @pl.when(s < EARLY)
@@ -305,6 +311,39 @@
             y_copy(4, it - 1).wait_recv()
             y_copy(7, it - 1).start()
 
+        @between(it + 3, EARLY, STEPS)
+        def _():
+            hidden_on(it + 3)
+
+        @between(it + 5, EARLY + 2, STEPS)
+        def _():
+            hidden_out(it + 5)
+
+        @between(it - 1, 0, STEPS)
+        def _():
+            s = it - 1
+            y_copy(7, s).wait_recv()
+            whole = project_far(s)
+
+            @pl.when(s < EARLY)
+            def _():
+                msg[s] = whole
+                exchange(0, s, lambda j: msg.at[s, j], r1.at[s, me])
+                r1[s, me] = msg[s, me]
+
+            @pl.when(s >= EARLY)
+            def _():
+                r2[s] = whole
+
+        @between(it + 2, 2, STEPS)
+        def _():
+            @pl.when(it + 2 >= EARLY)
+            def _():
+                arrived(x_recv.at[5, it + 2], rh)
+
+            near_send(it + 2)
+
+        late_and_early(it - 1, it - 4, work)
         late_and_early(it - 2, it - 5, back_on)
 
         @between(it - 2, 0, EARLY)
@@ -318,37 +357,6 @@
             exchange(1, s, lambda o: st2.at[s, o], r2.at[s, me])
             r2[s, me] = st2[s, me]
 
-        @between(it + 4, 2 * EARLY, STEPS)
-        def _():
-            hidden_on(it + 4)
-
-        @between(it + 6, 3 * EARLY, STEPS)
-        def _():
-            hidden_out(it + 6)
-
-        @between(it - 1, 0, STEPS)
-        def _():
-            s = it - 1
-            y_copy(7, s).wait_recv()
-            whole = project_far(s)
-
-            @pl.when(s < EARLY)
-            def _():
-                msg[s] = whole
-                exchange(0, s, lambda j: msg.at[s, j], r1.at[s, me])
-                r1[s, me] = msg[s, me]
-
-            @pl.when(s >= EARLY)
-            def _():
-                r2[s] = whole
-
-        @between(it + 2, EARLY, STEPS)
-        def _():
-            arrived(x_recv.at[5, it + 2], rh)
-            near_send(it + 2)
-
-        late_and_early(it - 1, it - 4, work)
-
         @between(it, 0, STEPS)
         def _():
             for kind in (2, 5, 6):
@@ -363,6 +371,8 @@
     def drain(s, carry):
         for kind in range(8):
             y_copy(kind, s).wait_send()
+        cache_copy(s).wait()
+        out_copy(s).wait()
         arrived(x_send.at[2, s], om)
         arrived(x_send.at[3, s], st4)
 
@@ -379,6 +389,24 @@
         return carry
 
     lax.fori_loop(0, STEPS, drain, 0)
+
+
+def hand_over(a, b, out, cache, a_held, b_held, sem):
+    parts = []
+    for s in range(0, STEPS, 2):
+        rows = pl.ds(s * SPAN_LEN, 2 * SPAN_LEN)
+        parts.append((a.at[rows], a_held.at[rows], out.at[rows]))
+        spans = pl.ds(s, 2)
+        parts.append((b.at[spans], b_held.at[spans], cache.at[spans]))
+    first = [pltpu.make_async_copy(p[0], p[1], sem.at[0, i]) for i, p in enumerate(parts)]
+    second = [pltpu.make_async_copy(p[1], p[2], sem.at[1, i]) for i, p in enumerate(parts)]
+    for copy in first:
+        copy.start()
+    for one, two in zip(first, second):
+        one.wait()
+        two.start()
+    for copy in second:
+        copy.wait()
 
 
 def trig_tables():
@@ -394,14 +422,15 @@
     dma = pltpu.SemaphoreType.DMA
     any_spec = pl.BlockSpec(memory_space=pl.ANY)
     vmem = pl.BlockSpec(memory_space=pltpu.VMEM)
-    return pl.pallas_call(
+    shapes = (
+        jax.ShapeDtypeStruct((STEPS * SPAN_LEN, GROUP * 128), BF),
+        jax.ShapeDtypeStruct((STEPS, SPAN_LEN, 256), BF),
+    )
+    results = pl.pallas_call(
         kernel,
-        out_shape=(
-            jax.ShapeDtypeStruct((STEPS * SPAN_LEN, GROUP * 128), BF),
-            jax.ShapeDtypeStruct((STEPS, SPAN_LEN, 256), BF),
-        ),
+        out_shape=shapes,
         in_specs=[pl.BlockSpec(memory_space=pltpu.SMEM)] * 3 + [any_spec] * 4 + [vmem],
-        out_specs=(vmem, vmem),
+        out_specs=(any_spec, any_spec),
         scratch_shapes=[
             v((STEPS, SPAN_LEN, 8 * CHUNK), BF),
             v((8 * CHUNK, GROUP * 128), BF),
@@ -424,7 +453,10 @@
             v((REPS, 16, HALF), BF),
             v((REPS, PIECE, 128), BF),
             v((REPS, BACK, 128), BF),
-            dma((31,)),
+            v((STEPS, SPAN_LEN, GROUP * 128), BF),
+            v((STEPS, SPAN_LEN, 256), BF),
+            dma((EARLY + 2 * LATE + 17,)),
+            dma((2, STEPS)),
             dma((8, STEPS)),
             dma((8, STEPS)),
             dma((6, STEPS)),
@@ -437,6 +469,13 @@
             flops=18_000_000_000, bytes_accessed=24_000_000, transcendentals=9_000_000
         ),
     )(prefix_len, owner, block_table.T, hidden, w_query, w_keyval, kv_pool, jnp.asarray(trig_tables()))
+    return pl.pallas_call(
+        hand_over,
+        out_shape=shapes,
+        in_specs=[any_spec] * 2,
+        out_specs=(any_spec, any_spec),
+        scratch_shapes=[v(shapes[0].shape, BF), v(shapes[1].shape, BF), dma((2, STEPS))],
+    )(*results)
 
 
 def solution(mesh):

time: 114 us -> 105 us (0.921)
  Pallas kernels: 109 us -> 104 us
  local copies, waits for them, and re-layouts: 4.13 us -> 0 us
    pallas_call x1 -> x2, Pallas kernels: 109 us -> 104 us  [the longest x1 101 us: body(): pl.pallas_call(kernel, out_shape=shapes, in_specs=[pl.BlockSpec(memory_sp...]
    unnamed x2 -> x0, local copies, waits for them, and re-layouts: 4.13 us -> none
where the time goes in v3:
time: 105 us; the launch traced here: 104 us
  Pallas kernels  104 us (99%)
    pallas_call x1, Pallas kernels, body(): pl.pallas_call(kernel, out_shape=shapes, in_specs=[pl.BlockSpec(memory_sp...  101 us
    pallas_call x1, Pallas kernels, body(): pl.pallas_call(hand_over, out_shape=shapes, in_specs=[any_spec] * 2, out_...  2.23 us

profile of v3, /device:TPU:0, one launch (start us, length us, event | category | flops | bytes accessed | tf_op | source)
XLA Modules:
  0.0 104.2 jit_solution(13330104434040901166)
XLA Ops:
  0.6 101.3 %shard_map.95 = (bf16[1024,512]{1,0:T(8,128)(2,1)}, bf16[8,128,256]{2,1,0:T(8,128)(2,1)}) custom-call(s32[128]{0:T(128)} %lens.1, s32[128]{0:T(128)} %owner.1, s32[16,128]{1,0:T(8,128)} %bitcast.1, bf16[1024,1024]{1,0:T(8,128)(2,1)} %hid.1, bf16[8192,512]{1,0:T(8,128)(2,1)} %wq_h.1, bf16[8192,256]{1,0:T(8,128)(2,1)} %wkv_h.1, bf16[128,128,256]{2,1,0:T(8,128)(2,1)} %pool_h.1, ...), custom_call_target="tpu_custom_call" | custom-call | flops 17999998976 | bytes 24000000 | tf_op jit(solution)/shard_map/pallas_call | solution.py:429
  102.0 2.2 %shard_map.96 = (bf16[1024,512]{1,0:T(8,128)(2,1)}, bf16[8,128,256]{2,1,0:T(8,128)(2,1)}) custom-call(bf16[1024,512]{1,0:T(8,128)(2,1)} %get-tuple-element.4.a, bf16[8,128,256]{2,1,0:T(8,128)(2,1)} %get-tuple-element.5.b), custom_call_target="tpu_custom_call" | custom-call | tf_op jit(solution)/shard_map/pallas_call | solution.py:472

commit v4 on v3

--- a/solution.py
+++ b/solution.py
@@ -40,10 +40,10 @@
 
 
 def kernel(
-    lens, owner, pages, hid, wq_h, wkv_h, pool_h, trig, out, cache,
-    gath, wq, wkv, pool, accq, acck, hv, rh, sth, msg, r1, st2, r2, om, r3, st4, r4,
-    scores, workh, work1, work3, outv, cachev,
-    local_sem, out_sem, y_send, y_recv, x_send, x_recv,
+    lens, owner, pages, hid, wq_h, wkv_h, pool_h, trig, back, cache,
+    gath, wq, wkv, pool, accq, acck, hv, rh, sth, msg, r1, st2, r2, om, r3, st4,
+    scores, workh, work1, work3, cachev,
+    local_sem, out_sem, hello, y_send, y_recv, x_send, x_recv,
 ):
     me = lax.axis_index("rep")
     tp = lax.axis_index("tp")
@@ -81,14 +81,15 @@
     for one in loads:
         one.start()
 
+    def along(dx, dz):
+        return (lax.rem(me // 4 + dx, 4) * 4 + lax.rem(lax.rem(me, 4) + dz, 4), tp)
+
     barrier = pltpu.get_barrier_semaphore()
-    for device in (up, down, sib):
+    for device in (up, down, sib, along(1, 0), along(3, 0), along(0, 1), along(0, 3)):
         pl.semaphore_signal(barrier, inc=1, device_id=device, device_id_type=MESH)
-    for peer in peers:
-        pl.semaphore_signal(barrier, inc=1, device_id=(peer, tp), device_id_type=MESH)
     for one in loads[:hidden_loads]:
         one.wait()
-    pl.semaphore_wait(barrier, 3 + REPS - 1)
+    pl.semaphore_wait(barrier, 7)
 
     def remote(src, dst, send, recv, device):
         return pltpu.make_async_remote_copy(
@@ -171,6 +172,10 @@
 
     near_send(0)
     near_send(1)
+    for n, (dx, dz) in enumerate([(1, 0), (0, 1), (0, 1)]):
+        for device in (along(dx, dz), along(3 * dx, 3 * dz)):
+            pl.semaphore_signal(hello.at[n], inc=1, device_id=device, device_id_type=MESH)
+        pl.semaphore_wait(hello.at[n], 2)
     lax.fori_loop(EARLY, EARLY + 2, lambda s, _: hidden_out(s), None)
     for one in loads[hidden_loads:]:
         one.wait()
@@ -210,9 +215,12 @@
     def cache_copy(s):
         return pltpu.make_async_copy(cachev.at[s], cache.at[s], out_sem.at[0, s])
 
-    def out_copy(s):
-        rows = pl.ds(pl.multiple_of(s * SPAN_LEN, SPAN_LEN), SPAN_LEN)
-        return pltpu.make_async_copy(outv.at[s], out.at[rows], out_sem.at[1, s])
+    def place(s):
+        rows = pl.ds(pl.multiple_of(s * SPAN_LEN + lax.rem(me, 4) * BACK, BACK), BACK)
+        return back.at[rows, pl.ds(pl.multiple_of(me // 4 * 128, 128), 128)]
+
+    def own_copy(s):
+        return pltpu.make_async_copy(st4.at[s, me], place(s), out_sem.at[1, s])
 
     def attend(s):
         row = owned(s)
@@ -276,15 +284,29 @@
         work3[...] = r3[s]
         for r in range(REPS):
             st4[s, r] = work3[owner[r * STEPS + s]]
-        exchange(3, s, lambda r: st4.at[s, r], r4.at[s, me])
-        r4[s, me] = st4[s, me]
+        exchange(3, s, lambda r: st4.at[s, r], place(s))
+        own_copy(s).start()
+
+    def settle(s):
+        for kind in range(8):
+            y_copy(kind, s).wait_send()
+        cache_copy(s).wait()
+        arrived(x_send.at[2, s], om)
+
+        @pl.when(s < EARLY)
+        def _():
+            arrived(x_send.at[0, s], msg)
+            arrived(x_send.at[1, s], st2)
+
+        @pl.when(s >= EARLY)
+        def _():
+            arrived(x_send.at[4, s], rh)
+            arrived(x_send.at[5, s], sth)
 
     def finish(s):
-        arrived(x_recv.at[3, s], r4)
-        whole = r4[s].reshape(ROWS, 128)
-        for h in range(GROUP):
-            outv[s, :, h * 128 : (h + 1) * 128] = whole[h * 128 : (h + 1) * 128]
-        out_copy(s).start()
+        own_copy(s).wait()
+        arrived(x_send.at[3, s], st4)
+        arrived(x_recv.at[3, s], st4)
 
     def work(s):
         @pl.when(s < EARLY)
@@ -294,6 +316,11 @@
         attend(s)
         exchange(2, s, lambda j: om.at[s, j], r3.at[s, me])
         r3[s, me] = om[s, me]
+
+    def far_on(s):
+        y_copy(3, s).wait_recv()
+        y_copy(4, s).wait_recv()
+        y_copy(7, s).start()
 
     def step(it, carry):
         @between(it, 0, STEPS)
@@ -305,11 +332,9 @@
             y_copy(4, it).start()
             y_copy(6, it).start()
 
-        @between(it - 1, 0, STEPS)
-        def _():
-            y_copy(3, it - 1).wait_recv()
-            y_copy(4, it - 1).wait_recv()
-            y_copy(7, it - 1).start()
+        @between(it - 1, 0, STEPS - 1)
+        def _():
+            far_on(it - 1)
 
         @between(it + 3, EARLY, STEPS)
         def _():
@@ -344,6 +369,10 @@
             near_send(it + 2)
 
         late_and_early(it - 1, it - 4, work)
+        @pl.when(it == STEPS - 1)
+        def _():
+            far_on(it)
+
         late_and_early(it - 2, it - 5, back_on)
 
         @between(it - 2, 0, EARLY)
@@ -363,41 +392,21 @@
                 y_copy(kind, it).wait_recv()
             project_near(it)
 
-        late_and_early(it - 3, it - 6, finish)
+        late_and_early(it - 2, it - 6, settle)
+        late_and_early(it - 3, it - 7, finish)
         return carry
 
     lax.fori_loop(0, STEPS + 3, step, 0)
 
-    def drain(s, carry):
-        for kind in range(8):
-            y_copy(kind, s).wait_send()
-        cache_copy(s).wait()
-        out_copy(s).wait()
-        arrived(x_send.at[2, s], om)
-        arrived(x_send.at[3, s], st4)
-
-        @pl.when(s < EARLY)
-        def _():
-            arrived(x_send.at[0, s], msg)
-            arrived(x_send.at[1, s], st2)
-
-        @pl.when(s >= EARLY)
-        def _():
-            arrived(x_send.at[4, s], rh)
-            arrived(x_send.at[5, s], sth)
-
-        return carry
-
-    lax.fori_loop(0, STEPS, drain, 0)
-
-
-def hand_over(a, b, out, cache, a_held, b_held, sem):
+
+def hand_over(back, fresh, out, cache, out_held, cache_held, sem):
     parts = []
     for s in range(0, STEPS, 2):
         rows = pl.ds(s * SPAN_LEN, 2 * SPAN_LEN)
-        parts.append((a.at[rows], a_held.at[rows], out.at[rows]))
-        spans = pl.ds(s, 2)
-        parts.append((b.at[spans], b_held.at[spans], cache.at[spans]))
+        parts.append((back.at[rows], out_held.at[rows], out.at[rows]))
+    for s in range(0, STEPS, 4):
+        spans = pl.ds(s, 4)
+        parts.append((fresh.at[spans], cache_held.at[spans], cache.at[spans]))
     first = [pltpu.make_async_copy(p[0], p[1], sem.at[0, i]) for i, p in enumerate(parts)]
     second = [pltpu.make_async_copy(p[1], p[2], sem.at[1, i]) for i, p in enumerate(parts)]
     for copy in first:
@@ -448,15 +457,14 @@
             v((STEPS, REPS, BACK, 128), BF),
             v((STEPS, REPS, BACK, 128), BF),
             v((STEPS, REPS, BACK, 128), BF),
-            v((STEPS, REPS, BACK, 128), BF),
             v((BLOCK, KEYS), F32),
             v((REPS, 16, HALF), BF),
             v((REPS, PIECE, 128), BF),
             v((REPS, BACK, 128), BF),
-            v((STEPS, SPAN_LEN, GROUP * 128), BF),
             v((STEPS, SPAN_LEN, 256), BF),
             dma((EARLY + 2 * LATE + 17,)),
             dma((2, STEPS)),
+            pltpu.SemaphoreType.REGULAR((3,)),
             dma((8, STEPS)),
             dma((8, STEPS)),
             dma((6, STEPS)),

time: 105 us -> 102 us (0.971)
  Pallas kernels: 104 us -> 101 us
    pallas_call x1, Pallas kernels: 101 us -> 98.7 us  [body(): pl.pallas_call(kernel, out_shape=shapes, in_specs=[pl.BlockSpec(memory_sp...]
where the time goes in v4:
time: 102 us
  Pallas kernels  101 us (99%)
    pallas_call x1, Pallas kernels, body(): pl.pallas_call(kernel, out_shape=shapes, in_specs=[pl.BlockSpec(memory_sp...  98.7 us
    pallas_call x1, Pallas kernels, body(): pl.pallas_call(hand_over, out_shape=shapes, in_specs=[any_spec] * 2, out_...  2.22 us

profile of v4, /device:TPU:0, one launch (start us, length us, event | category | flops | bytes accessed | tf_op | source)
XLA Modules:
  0.0 101.6 jit_solution(8077085514343804314)
XLA Ops:
  0.6 98.7 %shard_map.95 = (bf16[1024,512]{1,0:T(8,128)(2,1)}, bf16[8,128,256]{2,1,0:T(8,128)(2,1)}) custom-call(s32[128]{0:T(128)} %lens.1, s32[128]{0:T(128)} %owner.1, s32[16,128]{1,0:T(8,128)} %bitcast.1, bf16[1024,1024]{1,0:T(8,128)(2,1)} %hid.1, bf16[8192,512]{1,0:T(8,128)(2,1)} %wq_h.1, bf16[8192,256]{1,0:T(8,128)(2,1)} %wkv_h.1, bf16[128,128,256]{2,1,0:T(8,128)(2,1)} %pool_h.1, ...), custom_call_target="tpu_custom_call" | custom-call | flops 17999998976 | bytes 24000000 | tf_op jit(solution)/shard_map/pallas_call | solution.py:438
  99.4 2.2 %shard_map.96 = (bf16[1024,512]{1,0:T(8,128)(2,1)}, bf16[8,128,256]{2,1,0:T(8,128)(2,1)}) custom-call(bf16[1024,512]{1,0:T(8,128)(2,1)} %get-tuple-element.4.back, bf16[8,128,256]{2,1,0:T(8,128)(2,1)} %get-tuple-element.5.fresh), custom_call_target="tpu_custom_call" | custom-call | tf_op jit(solution)/shard_map/pallas_call | solution.py:480

commit v5 on v4

--- a/solution.py
+++ b/solution.py
@@ -344,6 +344,20 @@
         def _():
             hidden_out(it + 5)
 
+        @between(it, 0, STEPS)
+        def _():
+            for kind in (2, 5, 6):
+                y_copy(kind, it).wait_recv()
+            project_near(it)
+
+        @between(it + 2, 2, STEPS)
+        def _():
+            @pl.when(it + 2 >= EARLY)
+            def _():
+                arrived(x_recv.at[5, it + 2], rh)
+
+            near_send(it + 2)
+
         @between(it - 1, 0, STEPS)
         def _():
             s = it - 1
@@ -360,20 +374,12 @@
             def _():
                 r2[s] = whole
 
-        @between(it + 2, 2, STEPS)
-        def _():
-            @pl.when(it + 2 >= EARLY)
-            def _():
-                arrived(x_recv.at[5, it + 2], rh)
-
-            near_send(it + 2)
-
-        late_and_early(it - 1, it - 4, work)
         @pl.when(it == STEPS - 1)
         def _():
             far_on(it)
 
-        late_and_early(it - 2, it - 5, back_on)
+        late_and_early(it - 1, it - 3, work)
+        late_and_early(it - 2, it - 4, back_on)
 
         @between(it - 2, 0, EARLY)
         def _():
@@ -386,14 +392,8 @@
             exchange(1, s, lambda o: st2.at[s, o], r2.at[s, me])
             r2[s, me] = st2[s, me]
 
-        @between(it, 0, STEPS)
-        def _():
-            for kind in (2, 5, 6):
-                y_copy(kind, it).wait_recv()
-            project_near(it)
-
-        late_and_early(it - 2, it - 6, settle)
-        late_and_early(it - 3, it - 7, finish)
+        late_and_early(it - 2, it - 5, settle)
+        late_and_early(it - 3, it - 6, finish)
         return carry
 
     lax.fori_loop(0, STEPS + 3, step, 0)

time: 102 us -> 99.5 us (0.975)
  Pallas kernels: 101 us -> 98.7 us
    pallas_call x1, Pallas kernels: 98.7 us -> 96.4 us  [body(): pl.pallas_call(kernel, out_shape=shapes, in_specs=[pl.BlockSpec(memory_sp...]
where the time goes in v5:
time: 99.5 us; the launch traced here: 99.3 us
  Pallas kernels  98.7 us (99%)
    pallas_call x1, Pallas kernels, body(): pl.pallas_call(kernel, out_shape=shapes, in_specs=[pl.BlockSpec(memory_sp...  96.4 us
    pallas_call x1, Pallas kernels, body(): pl.pallas_call(hand_over, out_shape=shapes, in_specs=[any_spec] * 2, out_...  2.22 us

profile of v5, /device:TPU:0, one launch (start us, length us, event | category | flops | bytes accessed | tf_op | source)
XLA Modules:
  0.0 99.3 jit_solution(4211429985232110957)
XLA Ops:
  0.6 96.4 %shard_map.95 = (bf16[1024,512]{1,0:T(8,128)(2,1)}, bf16[8,128,256]{2,1,0:T(8,128)(2,1)}) custom-call(s32[128]{0:T(128)} %lens.1, s32[128]{0:T(128)} %owner.1, s32[16,128]{1,0:T(8,128)} %bitcast.1, bf16[1024,1024]{1,0:T(8,128)(2,1)} %hid.1, bf16[8192,512]{1,0:T(8,128)(2,1)} %wq_h.1, bf16[8192,256]{1,0:T(8,128)(2,1)} %wkv_h.1, bf16[128,128,256]{2,1,0:T(8,128)(2,1)} %pool_h.1, ...), custom_call_target="tpu_custom_call" | custom-call | flops 17999998976 | bytes 24000000 | tf_op jit(solution)/shard_map/pallas_call | solution.py:438
  97.1 2.2 %shard_map.96 = (bf16[1024,512]{1,0:T(8,128)(2,1)}, bf16[8,128,256]{2,1,0:T(8,128)(2,1)}) custom-call(bf16[1024,512]{1,0:T(8,128)(2,1)} %get-tuple-element.4.back, bf16[8,128,256]{2,1,0:T(8,128)(2,1)} %get-tuple-element.5.fresh), custom_call_target="tpu_custom_call" | custom-call | tf_op jit(solution)/shard_map/pallas_call | solution.py:480

commit v6 on v5

--- a/solution.py
+++ b/solution.py
@@ -322,63 +322,7 @@
         y_copy(4, s).wait_recv()
         y_copy(7, s).start()
 
-    def step(it, carry):
-        @between(it, 0, STEPS)
-        def _():
-            y_copy(0, it).wait_recv()
-            y_copy(3, it).start()
-            y_copy(5, it).start()
-            y_copy(1, it).wait_recv()
-            y_copy(4, it).start()
-            y_copy(6, it).start()
-
-        @between(it - 1, 0, STEPS - 1)
-        def _():
-            far_on(it - 1)
-
-        @between(it + 3, EARLY, STEPS)
-        def _():
-            hidden_on(it + 3)
-
-        @between(it + 5, EARLY + 2, STEPS)
-        def _():
-            hidden_out(it + 5)
-
-        @between(it, 0, STEPS)
-        def _():
-            for kind in (2, 5, 6):
-                y_copy(kind, it).wait_recv()
-            project_near(it)
-
-        @between(it + 2, 2, STEPS)
-        def _():
-            @pl.when(it + 2 >= EARLY)
-            def _():
-                arrived(x_recv.at[5, it + 2], rh)
-
-            near_send(it + 2)
-
-        @between(it - 1, 0, STEPS)
-        def _():
-            s = it - 1
-            y_copy(7, s).wait_recv()
-            whole = project_far(s)
-
-            @pl.when(s < EARLY)
-            def _():
-                msg[s] = whole
-                exchange(0, s, lambda j: msg.at[s, j], r1.at[s, me])
-                r1[s, me] = msg[s, me]
-
-            @pl.when(s >= EARLY)
-            def _():
-                r2[s] = whole
-
-        @pl.when(it == STEPS - 1)
-        def _():
-            far_on(it)
-
-        late_and_early(it - 1, it - 3, work)
+    def follow(it, carry):
         late_and_early(it - 2, it - 4, back_on)
 
         @between(it - 2, 0, EARLY)
@@ -393,10 +337,73 @@
             r2[s, me] = st2[s, me]
 
         late_and_early(it - 2, it - 5, settle)
-        late_and_early(it - 3, it - 6, finish)
+        late_and_early(it - 4, it - 7, finish)
         return carry
 
-    lax.fori_loop(0, STEPS + 3, step, 0)
+    def step(it, carry):
+        @between(it, 0, STEPS)
+        def _():
+            y_copy(0, it).wait_recv()
+            y_copy(3, it).start()
+            y_copy(5, it).start()
+            y_copy(1, it).wait_recv()
+            y_copy(4, it).start()
+            y_copy(6, it).start()
+
+        @between(it - 1, 0, STEPS - 1)
+        def _():
+            far_on(it - 1)
+
+        @between(it + 3, EARLY, STEPS)
+        def _():
+            hidden_on(it + 3)
+
+        @between(it + 5, EARLY + 2, STEPS)
+        def _():
+            hidden_out(it + 5)
+
+        @between(it, 0, STEPS)
+        def _():
+            for kind in (2, 5, 6):
+                y_copy(kind, it).wait_recv()
+            project_near(it)
+
+        @between(it + 2, 2, STEPS)
+        def _():
+            @pl.when(it + 2 >= EARLY)
+            def _():
+                arrived(x_recv.at[5, it + 2], rh)
+
+            near_send(it + 2)
+
+        @between(it - 1, 0, STEPS)
+        def _():
+            s = it - 1
+            y_copy(7, s).wait_recv()
+            whole = project_far(s)
+
+            @pl.when(s < EARLY)
+            def _():
+                msg[s] = whole
+                exchange(0, s, lambda j: msg.at[s, j], r1.at[s, me])
+                r1[s, me] = msg[s, me]
+
+            @pl.when(s >= EARLY)
+            def _():
+                r2[s] = whole
+
+        @pl.when(it == STEPS - 1)
+        def _():
+            far_on(it)
+
+        late_and_early(it - 1, it - 3, work)
+        last = STEPS - 1
+        lax.fori_loop(
+            jnp.where(it == last + 1, last, it), jnp.where(it == last, it, it + 1), follow, 0
+        )
+        return carry
+
+    lax.fori_loop(0, STEPS + 4, step, 0)
 
 
 def hand_over(back, fresh, out, cache, out_held, cache_held, sem):

time: 99.5 us -> 99.2 us (level)
  no operation moved by 1% of the time
where the time goes in v6:
time: 99.2 us; the launch traced here: 99 us
  Pallas kernels  98.3 us (99%)
    pallas_call x1, Pallas kernels, body(): pl.pallas_call(kernel, out_shape=shapes, in_specs=[pl.BlockSpec(memory_sp...  96.1 us
    pallas_call x1, Pallas kernels, body(): pl.pallas_call(hand_over, out_shape=shapes, in_specs=[any_spec] * 2, out_...  2.22 us

profile of v6, /device:TPU:0, one launch (start us, length us, event | category | flops | bytes accessed | tf_op | source)
XLA Modules:
  0.0 99.0 jit_solution(3281933902171744061)
XLA Ops:
  0.6 96.1 %shard_map.95 = (bf16[1024,512]{1,0:T(8,128)(2,1)}, bf16[8,128,256]{2,1,0:T(8,128)(2,1)}) custom-call(s32[128]{0:T(128)} %lens.1, s32[128]{0:T(128)} %owner.1, s32[16,128]{1,0:T(8,128)} %bitcast.1, bf16[1024,1024]{1,0:T(8,128)(2,1)} %hid.1, bf16[8192,512]{1,0:T(8,128)(2,1)} %wq_h.1, bf16[8192,256]{1,0:T(8,128)(2,1)} %wkv_h.1, bf16[128,128,256]{2,1,0:T(8,128)(2,1)} %pool_h.1, ...), custom_call_target="tpu_custom_call" | custom-call | flops 17999998976 | bytes 24000000 | tf_op jit(solution)/shard_map/pallas_call | solution.py:445
  96.7 2.2 %shard_map.96 = (bf16[1024,512]{1,0:T(8,128)(2,1)}, bf16[8,128,256]{2,1,0:T(8,128)(2,1)}) custom-call(bf16[1024,512]{1,0:T(8,128)(2,1)} %get-tuple-element.4.back, bf16[8,128,256]{2,1,0:T(8,128)(2,1)} %get-tuple-element.5.fresh), custom_call_target="tpu_custom_call" | custom-call | tf_op jit(solution)/shard_map/pallas_call | solution.py:487

commit v7 on v6

--- a/solution.py
+++ b/solution.py
@@ -221,6 +221,21 @@
 
     def own_copy(s):
         return pltpu.make_async_copy(st4.at[s, me], place(s), out_sem.at[1, s])
+
+    def result_out(s, begin):
+        count = BLOCK // BACK
+        for d in (6, 5, 7, 2, 3, 1, 4, 0):
+            j = begin + lax.rem(lax.rem(me, count) + d, count)
+
+            def send(j=j):
+                remote(
+                    om.at[s, j], r3.at[s, me], x_send.at[2, s], x_recv.at[2, s], (j, tp)
+                ).start()
+
+            if d:
+                send()
+            else:
+                pl.when(j != me)(send)
 
     def attend(s):
         row = owned(s)
@@ -263,6 +278,7 @@
             total = jnp.sum(total, axis=1, keepdims=True)
             done = (summed / total).astype(BF).reshape(BLOCK // BACK, BACK, 128)
             om[s, first // BACK : (first + BLOCK) // BACK] = done
+            result_out(s, first // BACK)
 
     def between(s, low, high):
         return pl.when((s >= low) & (s < high))
@@ -314,7 +330,6 @@
             arrived(x_recv.at[1, s], r1)
 
         attend(s)
-        exchange(2, s, lambda j: om.at[s, j], r3.at[s, me])
         r3[s, me] = om[s, me]
 
     def far_on(s):

time: 99.2 us -> 102 us (1.028)
  Pallas kernels: 98.3 us -> 102 us
    pallas_call x1, Pallas kernels: 96.1 us -> 99.3 us  [body(): pl.pallas_call(kernel, out_shape=shapes, in_specs=[pl.BlockSpec(memory_sp...]
where the time goes in v7:
time: 102 us
  Pallas kernels  102 us (100%)
    pallas_call x1, Pallas kernels, body(): pl.pallas_call(kernel, out_shape=shapes, in_specs=[pl.BlockSpec(memory_sp...  99.3 us
    pallas_call x1, Pallas kernels, body(): pl.pallas_call(hand_over, out_shape=shapes, in_specs=[any_spec] * 2, out_...  2.22 us

profile of v7, /device:TPU:0, one launch (start us, length us, event | category | flops | bytes accessed | tf_op | source)
XLA Modules:
  0.0 102.2 jit_solution(11973429391715100637)
XLA Ops:
  0.6 99.3 %shard_map.95 = (bf16[1024,512]{1,0:T(8,128)(2,1)}, bf16[8,128,256]{2,1,0:T(8,128)(2,1)}) custom-call(s32[128]{0:T(128)} %lens.1, s32[128]{0:T(128)} %owner.1, s32[16,128]{1,0:T(8,128)} %bitcast.1, bf16[1024,1024]{1,0:T(8,128)(2,1)} %hid.1, bf16[8192,512]{1,0:T(8,128)(2,1)} %wq_h.1, bf16[8192,256]{1,0:T(8,128)(2,1)} %wkv_h.1, bf16[128,128,256]{2,1,0:T(8,128)(2,1)} %pool_h.1, ...), custom_call_target="tpu_custom_call" | custom-call | flops 17999998976 | bytes 24000000 | tf_op jit(solution)/shard_map/pallas_call | solution.py:460
  100.0 2.2 %shard_map.96 = (bf16[1024,512]{1,0:T(8,128)(2,1)}, bf16[8,128,256]{2,1,0:T(8,128)(2,1)}) custom-call(bf16[1024,512]{1,0:T(8,128)(2,1)} %get-tuple-element.4.back, bf16[8,128,256]{2,1,0:T(8,128)(2,1)} %get-tuple-element.5.fresh), custom_call_target="tpu_custom_call" | custom-call | tf_op jit(solution)/shard_map/pallas_call | solution.py:502
